TPU v7x, 512 devices: a whole 4x4x16 slice. The times are simulated.
512 devices in a mesh: row: 32 (over x, y, core), col: 16 (over z).
Axes of the slice: x: 4, y: 4, z: 16, core: 2. Of those that a mesh axis runs over, the one named last changes fastest.
Arguments:
- descriptors: bfloat16 [32, 98304], P(None, ('row', 'col')), may hold values from -6 to 6
- densities: float32 [98304], P(('row', 'col')), may hold values from 0.25 to 4
- vectors: float32 [32, 98304], P(None, ('row', 'col')), may hold values from -6 to 6
Outputs:
- next_block: float32 [32, 98304], P(None, ('row', 'col'))
All inputs are finite; a program needn't handle non-finite values.
Results may differ from a plain program's by a relative error of at most 0.0036.
Values may be sent and summed in bfloat16 or wider, within the bound.
A program may use at most 64 MiB of HBM per device.

v0:
```python
import math

import jax
import jax.numpy as jnp
from jax import lax
from jax.sharding import Mesh
from jax.sharding import PartitionSpec as P

ROW = ("row_0", "row_1", "row_2")
ROW_COL = ("row_0", "row_1", "row_2", "col")


kernel_width = 8.0


def from_everyone(shard, axis):
    count = lax.axis_size(axis)
    return lax.all_to_all(
        jnp.broadcast_to(shard[None], (count, *shard.shape)), axis, 0, 0, tiled=True
    )


def laid_out(tiles, dim):
    shape = list(tiles.shape[1:])
    shape[dim] *= tiles.shape[0]
    return jnp.moveaxis(tiles, 0, dim).reshape(shape)


def gather_directly(shard, axis, dim):
    tiles = from_everyone(shard, axis)
    return laid_out(tiles, dim)


def turned_gather(arrays, axis, dims):
    turned = [jnp.moveaxis(a, dim, 0) for a, dim in zip(arrays, dims)]
    widths = [t[0].size for t in turned]
    both = jnp.concatenate([t.reshape(-1, w) for t, w in zip(turned, widths)], axis=1)
    filled = lax.all_gather(both, axis, axis=0, tiled=True)
    tiles = jnp.split(filled, [sum(widths[:k]) for k in range(1, len(widths))], axis=1)
    return tuple(
        (
            jnp.moveaxis(b.reshape(-1, *t.shape[1:]), 0, dim)
            for b, t, dim in zip(tiles, turned, dims)
        )
    )


def cut_along(shard, dim, count):
    before, after = (shard.shape[:dim], shard.shape[dim + 1 :])
    return jnp.moveaxis(shard.reshape(*before, count, -1, *after), dim, 0)


def sent_and_summed(shard, axis, dim):
    count = lax.axis_size(axis)
    tiles = lax.all_to_all(cut_along(shard, dim, count), axis, 0, 0, tiled=True)
    return jnp.sum(tiles, axis=0)


def side_by_side(arrays, axis, dim, along):
    ends, at = ([], 0)
    for a in arrays[:-1]:
        at += a.shape[along]
        ends.append(at)
    both = jnp.concatenate(arrays, axis=along)
    return tuple(jnp.split(sent_and_summed(both, axis, dim), ends, axis=along))


def over_copies(shard, axis):
    return from_everyone(shard, axis).sum(axis=0)


def one_axis_at_a_time(shard, axes):
    far, near = axes
    return over_copies(over_copies(shard, near), far)


def in_one(arrays, axis):
    flat, at, finished = (jnp.concatenate([a.reshape(-1) for a in arrays]), 0, [])
    running = one_axis_at_a_time(flat, axis)
    for a in arrays:
        finished.append(running[at : at + a.size].reshape(a.shape))
        at += a.size
    return tuple(finished)


def tile_terms(targets, target_norm, piece):
    piece_feat, piece_vals, piece_inv = piece
    piece_norm = jnp.sum(jnp.square(piece_feat.astype(jnp.float32)), axis=0)
    feature_dim, target_count = targets.shape
    span_rows = math.gcd(target_count, 512)
    block_count = target_count // span_rows
    blocks = targets.reshape(feature_dim, block_count, span_rows).transpose(1, 0, 2)
    norm_blocks = target_norm.reshape(block_count, span_rows)

    def tile_block(block_item):
        block_feat, block_norm = block_item
        inner_prod = lax.dot_general(
            block_feat, piece_feat, (((0,), (0,)), ((), ())), preferred_element_type=jnp.float32
        )
        kernel = jnp.exp(
            -(block_norm[:, None] + piece_norm[None, :] - 2.0 * inner_prod) / kernel_width
        ).astype(jnp.bfloat16)
        numerator = lax.dot_general(
            piece_vals, kernel, (((1,), (1,)), ((), ())), preferred_element_type=jnp.float32
        )
        degree = lax.dot_general(
            piece_inv, kernel, (((1,), (1,)), ((), ())), preferred_element_type=jnp.float32
        )
        return (numerator, degree)

    numerator, degree = lax.map(tile_block, (blocks, norm_blocks))
    numerator = numerator.transpose(1, 0, 2).reshape(piece_vals.shape[0], target_count)
    degree = degree.transpose(1, 0, 2).reshape(1, target_count)
    return (numerator, degree)


def accumulate(targets, vec_count):
    target_norm = jnp.sum(jnp.square(targets.astype(jnp.float32)), axis=0)

    def fold_piece(running, piece, start):
        numerator, degree = tile_terms(targets, target_norm, piece)
        return (numerator, degree)

    initial = (
        jnp.zeros((vec_count, targets.shape[1]), jnp.float32),
        jnp.zeros((1, targets.shape[1]), jnp.float32),
    )
    return (fold_piece, initial)


def per_device(descriptors, densities, vectors):
    highest = lax.Precision.HIGHEST
    vec_count = vectors.shape[0]
    weighted = (vectors / densities[None, :]).astype(jnp.bfloat16)
    inverse = (1.0 / densities).astype(jnp.bfloat16)[None, :]
    targets = gather_directly(descriptors, ROW, 1)
    fold_piece, initial = accumulate(targets, vec_count)
    partial_value = fold_piece(
        initial, turned_gather((descriptors, weighted, inverse), "col", (1, 1, 1)), jnp.int32(0)
    )
    numerator, degree = side_by_side((partial_value[0], partial_value[1]), ROW, 1, 0)
    diffused = numerator / degree
    samples_float = float(descriptors.shape[1] * lax.axis_size(ROW) * lax.axis_size("col"))
    coupling, diffused_gram, basis_gram = in_one(
        (
            jnp.dot(vectors, diffused.T, precision=highest),
            jnp.dot(diffused, diffused.T, precision=highest),
            jnp.dot(vectors, vectors.T, precision=highest),
        ),
        (("row_0", "row_1"), ("row_2", "col")),
    )
    remainder = diffused - jnp.dot(coupling.T, vectors, precision=highest) / samples_float
    cross_term = jnp.dot(coupling.T, coupling, precision=highest)
    basis_term = jnp.dot(
        coupling.T, jnp.dot(basis_gram, coupling, precision=highest), precision=highest
    )
    spread = (
        diffused_gram
        - 2.0 * cross_term / samples_float
        + basis_term / (samples_float * samples_float)
    )
    factor = jnp.linalg.cholesky(spread)
    solved = jax.scipy.linalg.solve_triangular(factor, remainder, lower=True)
    return math.sqrt(samples_float) * solved


def solution(mesh):
    finer = Mesh(
        mesh.devices.reshape(4, 4, 2, mesh.shape["col"]), ("row_0", "row_1", "row_2", "col")
    )
    placed = (P(None, ROW_COL), P(ROW_COL), P(None, ROW_COL))
    return jax.shard_map(
        per_device, mesh=finer, in_specs=placed, out_specs=P(None, ROW_COL), check_vma=False
    )
```

profile of v0, /device:TPU:1, one launch (start us, length us, event | category | flops | bytes accessed | tf_op | source)
XLA Modules:
  0.0 182.3 jit_solution(6465203450939220424)
XLA Ops:
  0.0 1.6 broadcast_in_dim.23
  1.6 10.4 %all-to-all-start = ((bf16[32,32,192]{2,1,0:T(8,128)(2,1)}), bf16[32,32,192]{2,1,0:T(8,128)(2,1)S(1)}, u32[]{:S(2)}, u32[]{:S(2)}) async-start(bf16[32,32,192]{2,1,0:T(8,128)(2,1)} %broadcast_in_dim.23), calls=%async_computation | async-start | bytes 1048576 | tf_op jit(solution)/shard_map/all_to_all | solution.py:18
  14.2 29.9 %all-gather = bf16[16,192,65]{1,2,0:T(8,128)(2,1)S(1)} all-gather(bf16[1,192,65]{1,2,0:T(8,128)(2,1)S(1)} %maximum_bitcast_fusion.1), channel_id=1, replica_groups=mesh['row_0'=4,'row_1'=4,'row_2'=2,'col'=16] {'col'}, dimensions={0}, use_global_device_ids=true | all-gather | bytes 424320 | tf_op jit(solution)/shard_map/all_gather | solution.py:38
  46.5 43.8 %while.12 = (s32[]{:T(128)}, f32[12,32,512]{2,1,0:T(8,128)S(1)}, f32[12,1,512]{2,1,0:T(1,128)S(1)}, f32[12,512]{1,0:T(8,128)S(1)}, f32[3072]{0:T(1024)S(1)}, /*i...) while((s32[]{:T(128)}, f32[12,32,512]{2,1,0:T(8,128)S(1)}, ...), condition=%wide.region_3.4_spmd, body=%wide.region_2.3_spmd.sunk | while | flops 213909504 | bytes 9961589 | solution.py:111
  46.5 1.7 exponential_convert_fusion.2
  48.2 1.0 fusion.47
  49.2 0.9 fusion.48
  50.1 1.7 exponential_convert_fusion.2
  51.8 1.0 fusion.47
  52.8 0.9 fusion.48
  53.8 1.7 exponential_convert_fusion.2
  55.5 1.0 fusion.47
  56.5 0.9 fusion.48
  57.5 1.7 exponential_convert_fusion.2
  59.1 1.0 fusion.47
  60.2 0.9 fusion.48
  61.1 1.7 exponential_convert_fusion.2
  62.8 1.0 fusion.47
  63.8 0.9 fusion.48
  64.8 1.7 exponential_convert_fusion.2
  66.4 1.0 fusion.47
  67.5 0.9 fusion.48
  68.4 1.7 exponential_convert_fusion.2
  70.1 1.0 fusion.47
  71.1 0.9 fusion.48
  72.1 1.7 exponential_convert_fusion.2
  73.7 1.0 fusion.47
  74.8 0.9 fusion.48
  75.7 1.7 exponential_convert_fusion.2
  77.4 1.0 fusion.47
  78.4 0.9 fusion.48
  79.4 1.7 exponential_convert_fusion.2
  81.0 1.0 fusion.47
  82.1 0.9 fusion.48
  83.0 1.7 exponential_convert_fusion.2
  84.7 1.0 fusion.47
  85.7 0.9 fusion.48
  86.7 1.7 exponential_convert_fusion.2
  88.4 1.0 fusion.47
  89.4 0.9 fusion.48
  91.6 1.7 copy.49
  93.3 14.3 %all-to-all-start.1 = ((f32[32,33,192]{2,1,0:T(8,128)}), f32[32,33,192]{2,1,0:T(8,128)S(1)}, u32[]{:S(2)}, u32[]{:S(2)}) async-start(f32[32,33,192]{2,1,0:T(8,128)} %copy.49), calls=%async_computation.1 | async-start | bytes 2621440 | tf_op jit(solution)/shard_map/all_to_all | solution.py:55
  107.9 19.5 %all-to-all-done.1 = f32[32,33,192]{2,1,0:T(8,128)S(1)} async-done(((f32[32,33,192]{2,1,0:T(8,128)}), f32[32,33,192]{2,1,0:T(8,128)S(1)}, u32[]{:S(2)}, u32[]{:S(2)}) %all-to-all-start.1) | async-done | bytes 811040 | tf_op jit(solution)/shard_map/all_to_all | solution.py:55
  128.3 33.9 %all_to_all.22 = f32[32,1,3072]{2,1,0:T(1,128)S(1)} all-to-all(f32[32,1,3072]{2,1,0:T(1,128)S(1)} %broadcast_in_dim.40), channel_id=1, replica_groups=mesh['row_0'=4,'row_1'=4,'row_2'=2,'col'=16] {'row_2','col'}, dimensions={0} | all-to-all | bytes 786432 | tf_op jit(solution)/shard_map/all_to_all | solution.py:18
  162.5 10.9 %all_to_all.23 = f32[16,1,3072]{2,1,0:T(1,128)S(1)} all-to-all(f32[16,1,3072]{2,1,0:T(1,128)S(1)} %broadcast_in_dim.41), channel_id=1, replica_groups=mesh['row_0'=4,'row_1'=4,'row_2'=2,'col'=16] {'row_0','row_1'}, dimensions={0} | all-to-all | bytes 393216 | tf_op jit(solution)/shard_map/all_to_all | solution.py:18
  174.8 2.9 %cholesky.16 = f32[32,32]{1,0:T(8,128)S(1)} custom-call(f32[32,32]{1,0:T(8,128)S(1)} %fusion.11), custom_call_target="Cholesky" | custom-call | tf_op jit(solution)/shard_map/jit(cholesky)/cholesky | solution.py:162
  179.0 2.4 %custom-call.7 = f32[1,32,32]{1,2,0:T(8,128)S(1)} custom-call(f32[1,32,32]{2,1,0:T(8,128)S(1)} %fusion.9), custom_call_target="InvertDiagBlocksLowerTriangular" | custom-call | tf_op jit(solution)/shard_map/jit(_solve_triangular)/triangular_solve | solution.py:163
  181.5 0.9 convolution_multiply_fusion
  (64 shorter events, 9.9 us)
Async XLA Ops:
  1.6 43.4 %all-to-all-start = ((bf16[32,32,192]{2,1,0:T(8,128)(2,1)}), bf16[32,32,192]{2,1,0:T(8,128)(2,1)S(1)}, u32[]{:S(2)}, u32[]{:S(2)}) async-start(bf16[32,32,192]{2,1,0:T(8,128)(2,1)} %broadcast_in_dim.23), calls=%async_computation | async-start | bytes 1048576 | tf_op jit(solution)/shard_map/all_to_all | solution.py:18
  91.5 16.1 %copy-start = (f32[32,192]{1,0:T(8,128)S(1)}, f32[32,192]{1,0:T(8,128)}, u32[]{:S(2)}) copy-start(f32[32,192]{1,0:T(8,128)} %param.7) | copy-start | bytes 73732
  93.3 34.1 %all-to-all-start.1 = ((f32[32,33,192]{2,1,0:T(8,128)}), f32[32,33,192]{2,1,0:T(8,128)S(1)}, u32[]{:S(2)}, u32[]{:S(2)}) async-start(f32[32,33,192]{2,1,0:T(8,128)} %copy.49), calls=%async_computation.1 | async-start | bytes 2621440 | tf_op jit(solution)/shard_map/all_to_all | solution.py:55
where the time goes:
time: 183 us; the launch traced here: 182 us
  blocking collectives  74.7 us (41%)
  matrix products  45.7 us (25%)
  starting transfers between devices  24.7 us (13%)
  waiting for transfers between devices  19.5 us (11%)
  other arithmetic  9.74 us (5%)
  local copies, waits for them, and re-layouts  7.53 us (4%)
    all_to_all x2, blocking collectives, from_everyone(): lax.all_to_all(jnp.broadcast_to(shard[None], (count, *shard.shape)), axis...  44.8 us
    all_gather x1, blocking collectives, turned_gather(): filled = lax.all_gather(both, axis, axis=0, tiled=True)  29.9 us
    dot_general x12, matrix products, tile_block(): lax.dot_general(block_feat, piece_feat, (((0,), (0,)), ((), ())), preferr...  19.9 us
    all_to_all x1, waiting for transfers between devices, sent_and_summed(): tiles = lax.all_to_all(cut_along(shard, dim, count), axis, 0, 0, tiled=True)  19.5 us
    all_to_all x1, starting transfers between devices, sent_and_summed(): tiles = lax.all_to_all(cut_along(shard, dim, count), axis, 0, 0, tiled=True)  14.3 us
    dot_general x12, matrix products, tile_block(): lax.dot_general(piece_vals, kernel, (((1,), (1,)), ((), ())), preferred_e...  12.5 us
    dot_general x12, matrix products, tile_block(): lax.dot_general(piece_inv, kernel, (((1,), (1,)), ((), ())), preferred_el...  11.2 us
    all_to_all x1, starting transfers between devices, from_everyone(): lax.all_to_all(jnp.broadcast_to(shard[None], (count, *shard.shape)), axis...  10.4 us
  transfers between devices with their start and end apart: 2, of which 1 were waited for; matrix products, arithmetic and copies ran while one was open for 2% of the time, Pallas kernels for 0%

commit v1 on v0

v1 whole, which is shorter than its diff:
```python
import functools
import math

import jax
import jax.numpy as jnp
from jax import lax
from jax.experimental import pallas as pl
from jax.experimental.pallas import tpu as pltpu
from jax.sharding import PartitionSpec as P

MESH = pl.DeviceIdType.MESH
HIGHEST = lax.Precision.HIGHEST
F32, BF16 = jnp.float32, jnp.bfloat16

BLOCK = 192
PLANE = 16
DEPTH = 16
EXPONENT = math.log2(math.e) / 4.0


def norm_rows(x):
    half = 0.5 * jnp.sum(x * x, axis=0, keepdims=True)
    rest = jnp.broadcast_to(half, (16, half.shape[1]))
    at = lax.broadcasted_iota(jnp.int32, rest.shape, 0)
    rows = jnp.zeros_like(rest)
    for k in range(3):
        piece = rest.astype(BF16).astype(F32)
        rest = rest - piece
        rows = jnp.where(at == k, -piece, rows)
    return rows


def unit_rows(width):
    at = lax.broadcasted_iota(jnp.int32, (16, width), 0)
    return jnp.where(at < 3, 1.0, 0.0)


def lower_inverse(spread):
    n = spread.shape[0]
    at_row = lax.broadcasted_iota(jnp.int32, (n, 2 * n), 0)
    at_col = lax.broadcasted_iota(jnp.int32, (n, 2 * n), 1)
    both = jnp.concatenate([spread, spread], axis=1)
    work = jnp.where(at_col < n, both, jnp.where(at_col - n == at_row, 1.0, 0.0))
    for k in range(n):
        pivot_row = work[k : k + 1, :]
        inverse = lax.rsqrt(work[k : k + 1, k : k + 1])
        pivot_row = pivot_row * inverse
        column = work[:, k : k + 1] * inverse
        work = jnp.where(
            at_row > k, work - column * pivot_row, jnp.where(at_row == k, pivot_row, work)
        )
    return work[:, n:]


def kernel(
    desc_ref, dens_ref, vec_ref, out_ref,
    ring, sib, feats, tgt, wts, acc, parts_out, parts_in, held, tiles, slices_in, sums_in, total_in,
    ring_s, ring_r, sib_s, sib_r, tgt_s, tgt_r, part_s, part_r, ga_s, ga_r, gb_s, gb_r, gc_s, gc_r,
):
    row, z = lax.axis_index("row"), lax.axis_index("col")
    p, c = row // 2, row % 2
    other = 1 - c
    up, down = (z + 1) % DEPTH, (z + DEPTH - 1) % DEPTH
    half = p // 8
    samples = float(BLOCK * PLANE * DEPTH * 2)

    barrier = pltpu.get_barrier_semaphore()

    def greet(device):
        pl.semaphore_signal(barrier, inc=1, device_id=device, device_id_type=MESH)

    def greet_near(k, _):
        greet((((p + k) % PLANE) * 2 + c, z))
        greet((row, (z + k) % DEPTH))
        return 0

    lax.fori_loop(1, 16, greet_near, 0)

    def greet_half(k, _):
        greet(((half * 8 + k) * 2 + other, z))
        return 0

    lax.fori_loop(0, 8, greet_half, 0)
    greet((p * 2 + other, down))

    x = desc_ref[...].astype(F32)
    pieces = norm_rows(x)
    units = unit_rows(BLOCK)
    pad = lambda v: jnp.concatenate([v, jnp.zeros((v.shape[0], 256 - BLOCK), v.dtype)], axis=1)
    source = pad(jnp.concatenate([x, pieces, units], axis=0))
    later = pltpu.roll(source, 160, 1)
    packed = jnp.concatenate([source[:, :128], later[:, :128]], axis=0).T[:96]
    inverse = 1.0 / dens_ref[...]
    at16 = lax.broadcasted_iota(jnp.int32, (16, BLOCK), 0)
    vec = vec_ref[...]
    cols = pad(
        jnp.concatenate(
            [vec / dens_ref[...], jnp.where(at16 == 0, jnp.broadcast_to(inverse, (16, BLOCK)), 0.0)],
            axis=0,
        )
    )
    for d in range(2):
        ring[d, 0, 0:96] = packed.astype(BF16)
        ring[d, 0, 96:144] = cols[:, :128].astype(BF16)
        tail = cols[:, 128:]
        ring[d, 0, 144:192] = (pltpu.roll(tail, 64, 1) if d else tail).astype(BF16)
    sib[0, 0] = ring[0, 0]
    target = pad(jnp.concatenate([x, pieces], axis=0))
    odd = (p % 2) == 1
    tail = target[:, 128:]
    feats[p, 0:48] = target[:, :128].astype(BF16)
    feats[p, 48:96] = jnp.where(odd, pltpu.roll(tail, 64, 1), tail).astype(BF16)

    pl.semaphore_wait(barrier, 39)

    def ring_copy(d, r):
        if d == 0:
            device = (row, down)
        else:
            device = (p * 2 + jnp.where(r == 7, other, c), up)
        return pltpu.make_async_remote_copy(
            src_ref=ring.at[d, r], dst_ref=ring.at[d, r + 1],
            send_sem=ring_s.at[d, r], recv_sem=ring_r.at[d, r + 1],
            device_id=device, device_id_type=MESH,
        )

    def sib_copy(d, r):
        return pltpu.make_async_remote_copy(
            src_ref=ring.at[d, r], dst_ref=sib.at[d, r],
            send_sem=sib_s.at[d, r], recv_sem=sib_r.at[d, r],
            device_id=(p * 2 + other, z), device_id_type=MESH,
        )

    def tgt_copy(k):
        q = (p + k) % PLANE
        return pltpu.make_async_remote_copy(
            src_ref=feats.at[p], dst_ref=feats.at[p],
            send_sem=tgt_s.at[k], recv_sem=tgt_r.at[k],
            device_id=(q * 2 + c, z), device_id_type=MESH,
        )

    ring_copy(0, 0).start()
    ring_copy(1, 0).start()
    sib_copy(1, 0).start()

    def send_tgt(k, _):
        tgt_copy(k).start()
        return 0

    lax.fori_loop(1, 16, send_tgt, 0)
    acc[...] = jnp.zeros_like(acc)

    def wait_tgt(k, _):
        q = (p + PLANE - k) % PLANE
        pltpu.make_async_remote_copy(
            src_ref=feats.at[q], dst_ref=feats.at[q],
            send_sem=tgt_s.at[k], recv_sem=tgt_r.at[k],
            device_id=(q * 2 + c, z), device_id_type=MESH,
        ).wait_recv()
        return 0

    lax.fori_loop(1, 16, wait_tgt, 0)

    unit_tile = unit_rows(128).astype(BF16)
    zeros = jnp.zeros((64, 128), BF16)

    def build_tgt(pair, _):
        first, second = 2 * pair, 2 * pair + 1
        tile3 = (
            feats[first, 0:48],
            feats[second, 0:48],
            feats[first, 48:96] + feats[second, 48:96],
        )
        for t in range(3):
            tiles[3 * pair + t] = jnp.concatenate(
                [tile3[t][:32], unit_tile, tile3[t][32:48], zeros], axis=0
            )
        return 0

    lax.fori_loop(0, 8, build_tgt, 0)
    for k in range(12):
        tgt[k] = jnp.concatenate([tiles[2 * k], tiles[2 * k + 1]], axis=1)

    def unpack(first, second, base):
        for s, block in ((0, first), (1, second)):
            packed = block[0:96]
            held[base + 128 * s : base + 128 * s + 96, :] = packed
            packed = pltpu.roll(packed.astype(F32), 64, 1).astype(BF16)
            held[base + 128 * s + 96 : base + 128 * s + 128, :] = packed[0:32]
            held[base + 256 + 64 * s : base + 320 + 64 * s, :] = packed[32:96]
        wts[:, base : base + 128] = first[96:144]
        wts[:, base + 128 : base + 256] = second[96:144]
        wts[:, base + 256 : base + 384] = first[144:192] + second[144:192]

    def step(b, _):
        for d in range(2):
            ring_copy(d, b).wait_recv()

        @pl.when(b < 7)
        def _():
            for d in range(2):
                ring_copy(d, b + 1).start()
            for d in range(2):
                sib_copy(d, b + 1).start()

        @pl.when(b > 0)
        def _():
            sib_copy(0, b).wait_recv()

        sib_copy(1, b).wait_recv()
        unpack(ring[0, b + 1], ring[1, b + 1], 0)
        unpack(sib[0, b], sib[1, b], 384)
        rows = held[...]
        weights = wts[...]

        kernels, inner = {}, {}
        for k in range(14):
            if k < 12:
                inner[k] = jnp.dot(rows, tgt[k], preferred_element_type=F32)
            if 0 <= k - 1 < 12:
                kernels[k - 1] = jnp.exp2(inner.pop(k - 1) * F32(EXPONENT)).astype(BF16)
            if 0 <= k - 2 < 12:
                acc[k - 2] += jnp.dot(weights, kernels.pop(k - 2), preferred_element_type=F32)
        return 0

    lax.fori_loop(0, 8, step, 0)

    for pair in range(8):
        tile3 = []
        for t in range(3):
            tile = 3 * pair + t
            tile3.append(acc[tile // 2, :, (tile % 2) * 128 : (tile % 2) * 128 + 128].astype(BF16))
        for s in range(2):
            parts_out[2 * pair + s, 0:48] = tile3[s]
            parts_out[2 * pair + s, 48:96] = tile3[2]

    def part_copy(k):
        q = (p + k) % PLANE
        return pltpu.make_async_remote_copy(
            src_ref=parts_out.at[q], dst_ref=parts_in.at[k],
            send_sem=part_s.at[k], recv_sem=part_r.at[k],
            device_id=(q * 2 + c, z), device_id_type=MESH,
        )

    def send_part(k, _):
        part_copy(k).start()
        return 0

    lax.fori_loop(1, 16, send_part, 0)
    sums = parts_out[p].astype(F32)
    for k in range(1, 16):
        part_copy(k).wait_recv()
        sums = sums + parts_in[k].astype(F32)
    tail = sums[48:96]
    tail = jnp.where(odd, pltpu.roll(tail, 64, 1), tail)
    sums = jnp.concatenate([sums[0:48], tail], axis=1)[:, :BLOCK]
    diffused = sums[0:32] / sums[32:33]

    stacked = jnp.concatenate([vec, diffused], axis=0)
    gram = lax.dot_general(
        stacked, stacked, (((1,), (1,)), ((), ())), precision=HIGHEST, preferred_element_type=F32
    )
    gram = jnp.concatenate([gram, jnp.zeros((64, 64), F32)], axis=1)
    slices = slices_in.at[1]
    for j in range(8):
        slices[j] = gram[8 * j : 8 * j + 8]

    def ga_copy(k):
        q = (p + k) % PLANE
        return pltpu.make_async_remote_copy(
            src_ref=slices_in.at[1, q % 8], dst_ref=slices_in.at[0, k],
            send_sem=ga_s.at[k], recv_sem=ga_r.at[k],
            device_id=(q * 2 + c, z), device_id_type=MESH,
        )

    def send_ga(k, _):
        ga_copy(k).start()
        return 0

    lax.fori_loop(1, 16, send_ga, 0)
    part = slices_in[1, p % 8]
    for k in range(1, 16):
        ga_copy(k).wait_recv()
        part = part + slices_in[0, k]
    sums_in[0] = part

    def gb_copy(k):
        return pltpu.make_async_remote_copy(
            src_ref=sums_in.at[0], dst_ref=sums_in.at[k],
            send_sem=gb_s.at[k], recv_sem=gb_r.at[k],
            device_id=(row, (z + k) % DEPTH), device_id_type=MESH,
        )

    def send_gb(k, _):
        gb_copy(k).start()
        return 0

    lax.fori_loop(1, 16, send_gb, 0)
    for k in range(1, 16):
        gb_copy(k).wait_recv()
        part = part + sums_in[k]

    mine = p % 8
    total_in[c, mine] = part

    def gc_copy(s, k):
        q = half * 8 + (mine + k) % 8
        core = c if s == 0 else other
        return pltpu.make_async_remote_copy(
            src_ref=total_in.at[c, mine], dst_ref=total_in.at[c, mine],
            send_sem=gc_s.at[s, k], recv_sem=gc_r.at[s, k],
            device_id=(q * 2 + core, z), device_id_type=MESH,
        )

    def gc_recv(s, k):
        slot = (mine + 8 - k) % 8
        core = c if s == 0 else other
        return pltpu.make_async_remote_copy(
            src_ref=total_in.at[core, slot], dst_ref=total_in.at[core, slot],
            send_sem=gc_s.at[s, k], recv_sem=gc_r.at[s, k],
            device_id=(row, z), device_id_type=MESH,
        )

    def send_gc(k, _):
        gc_copy(1, k).start()

        @pl.when(k > 0)
        def _():
            gc_copy(0, k).start()

        return 0

    lax.fori_loop(0, 8, send_gc, 0)

    def wait_gc(k, _):
        gc_recv(1, k).wait_recv()

        @pl.when(k > 0)
        def _():
            gc_recv(0, k).wait_recv()

        return 0

    lax.fori_loop(0, 8, wait_gc, 0)
    total = (total_in[0] + total_in[1]).reshape(64, 128)
    basis, coupling, square = total[:32, :32], total[:32, 32:64], total[32:, 32:64]
    dot_t = lambda a, b: lax.dot_general(
        a, b, (((0,), (0,)), ((), ())), precision=HIGHEST, preferred_element_type=F32
    )
    mixed = jnp.dot(basis, coupling, precision=HIGHEST, preferred_element_type=F32)
    spread = square + dot_t(
        coupling, mixed * (1.0 / (samples * samples)) - coupling * (2.0 / samples)
    )
    remainder = diffused - dot_t(coupling, vec) * (1.0 / samples)
    factor = lower_inverse(spread)
    out_ref[...] = math.sqrt(samples) * jnp.dot(
        factor, remainder, precision=HIGHEST, preferred_element_type=F32
    )

    for d in range(2):
        def wait_ring(r, _):
            ring_copy(d, r).wait_send()
            return 0

        lax.fori_loop(0, 8, wait_ring, 0)

        def wait_sib(r, _):
            sib_copy(d, r).wait_send()
            return 0

        lax.fori_loop(1 - d, 8, wait_sib, 0)

    def wait_sent(k, _):
        tgt_copy(k).wait_send()
        part_copy(k).wait_send()
        ga_copy(k).wait_send()
        gb_copy(k).wait_send()
        return 0

    lax.fori_loop(1, 16, wait_sent, 0)

    def wait_gc_sent(k, _):
        gc_copy(1, k).wait_send()

        @pl.when(k > 0)
        def _():
            gc_copy(0, k).wait_send()

        return 0

    lax.fori_loop(0, 8, wait_gc_sent, 0)


def per_device(descriptors, densities, vectors):
    dma = pltpu.SemaphoreType.DMA
    return pl.pallas_call(
        kernel,
        out_shape=jax.ShapeDtypeStruct((32, BLOCK), F32),
        in_specs=[pl.BlockSpec(memory_space=pltpu.VMEM)] * 3,
        out_specs=pl.BlockSpec(memory_space=pltpu.VMEM),
        scratch_shapes=[
            pltpu.VMEM((2, 9, 192, 128), BF16),
            pltpu.VMEM((2, 8, 192, 128), BF16),
            pltpu.VMEM((16, 96, 128), BF16),
            pltpu.VMEM((12, 128, 256), BF16),
            pltpu.VMEM((48, 768), BF16),
            pltpu.VMEM((12, 48, 256), F32),
            pltpu.VMEM((16, 96, 128), BF16),
            pltpu.VMEM((16, 96, 128), BF16),
            pltpu.VMEM((768, 128), BF16),
            pltpu.VMEM((24, 128, 128), BF16),
            pltpu.VMEM((2, 16, 8, 128), F32),
            pltpu.VMEM((16, 8, 128), F32),
            pltpu.VMEM((2, 8, 8, 128), F32),
            dma((2, 9)), dma((2, 9)), dma((2, 8)), dma((2, 8)),
            dma((16,)), dma((16,)), dma((16,)), dma((16,)),
            dma((16,)), dma((16,)), dma((16,)), dma((16,)),
            dma((2, 8)), dma((2, 8)),
        ],
        compiler_params=pltpu.CompilerParams(
            collective_id=0, has_side_effects=True, vmem_limit_bytes=48 << 20
        ),
    )(descriptors, densities.reshape(1, BLOCK), vectors)


def solution(mesh):
    placed = P(None, ("row", "col"))
    return jax.shard_map(
        per_device,
        mesh=mesh,
        in_specs=(placed, P(("row", "col")), placed),
        out_specs=placed,
        check_vma=False,
    )
```

time: 183 us -> 85.3 us (0.47)
  Pallas kernels: 0 us -> 82.3 us
  blocking collectives: 74.7 us -> 0 us
  matrix products: 45.7 us -> 0 us
  starting transfers between devices: 24.7 us -> 0 us
  waiting for transfers between devices: 19.5 us -> 0 us
  other arithmetic: 9.74 us -> 0 us
  local copies, waits for them, and re-layouts: 7.53 us -> 2.77 us
    pallas_call x0 -> x1, Pallas kernels: none -> 82.3 us  [per_device(): pl.pallas_call(kernel, out_shape=jax.ShapeDtypeStruct((32, BLOCK), F32),...]
    all_to_all x2 -> x0, blocking collectives: 44.8 us -> none  [from_everyone(): lax.all_to_all(jnp.broadcast_to(shard[None], (count, *shard.shape)), axis...]
    dot_general x43 -> x0, matrix products: 44.8 us -> none  [the longest x12 19.9 us: tile_block(): lax.dot_general(block_feat, piece_feat, (((0,), (0,)), ((), ())), preferr...]
    all_gather x1 -> x0, blocking collectives: 29.9 us -> none  [turned_gather(): filled = lax.all_gather(both, axis, axis=0, tiled=True)]
    all_to_all x2 -> x0, starting transfers between devices: 24.7 us -> none  [the longest x1 14.3 us: sent_and_summed(): tiles = lax.all_to_all(cut_along(shard, dim, count), axis, 0, 0, tiled=True)]
    all_to_all x2 -> x0, waiting for transfers between devices: 19.5 us -> none  [the longest x1 19.5 us: sent_and_summed(): tiles = lax.all_to_all(cut_along(shard, dim, count), axis, 0, 0, tiled=True)]
    another operation x5 -> x0, other arithmetic: 6.68 us -> none  [the longest x3 3.6 us: per_device(): factor = jnp.linalg.cholesky(spread)]
    transpose x5 -> x0, local copies, waits for them, and re-layouts: 2.52 us -> none  [the longest x1 1.71 us: cut_along(): return jnp.moveaxis(shard.reshape(*before, count, -1, *after), dim, 0)]
  transfers between devices with their start and end apart: 2 -> 0, of which waited for: 1 -> 0; matrix products, arithmetic and copies ran while one was open for 2% -> 0% of each run, Pallas kernels for 0% -> 0%
where the time goes in v1:
time: 85.3 us; the launch traced here: 85.1 us
  Pallas kernels  82.3 us (96%)
  local copies, waits for them, and re-layouts  2.77 us (3%)
    pallas_call x1, Pallas kernels, per_device(): pl.pallas_call(kernel, out_shape=jax.ShapeDtypeStruct((32, BLOCK), F32),...  82.3 us
    unnamed x7, local copies, waits for them, and re-layouts  2.77 us

profile of v1, /device:TPU:1, one launch (start us, length us, event | category | flops | bytes accessed | tf_op | source)
XLA Modules:
  0.0 85.1 jit_solution(11455349045415225840)
XLA Ops:
  0.0 0.0 copy-start.2
  0.0 0.7 copy-done.2
  0.7 0.0 copy-start
  0.7 0.8 copy-done
  1.4 0.0 copy-start.1
  1.4 0.7 copy-done.1
  2.2 82.3 %shard_map.37 = f32[32,192]{1,0:T(8,128)S(1)} custom-call(bf16[32,192]{1,0:T(8,128)(2,1)S(1)} %copy-done.1, f32[1,192]{1,0:T(1,128)S(1)} %bitcast.1, f32[32,192]{1,0:T(8,128)S(1)} %copy-done), custom_call_target="tpu_custom_call" | custom-call | tf_op jit(solution)/shard_map/pallas_call | solution.py:396
  84.5 0.6 copy.5
Async XLA Ops:
  0.0 0.7 copy-start.2
  0.7 0.8 copy-start
  1.4 0.7 copy-start.1

commit v2 on v1

v2 whole, which is shorter than its diff:
```python
import functools
import math

import jax
import jax.numpy as jnp
from jax import lax
from jax.experimental import pallas as pl
from jax.experimental.pallas import tpu as pltpu
from jax.sharding import PartitionSpec as P

MESH = pl.DeviceIdType.MESH
HIGHEST = lax.Precision.HIGHEST
F32, BF16 = jnp.float32, jnp.bfloat16

BLOCK = 192
PLANE = 16
DEPTH = 16
EXPONENT = math.log2(math.e) / 4.0


def norm_rows(x):
    half = 0.5 * jnp.sum(x * x, axis=0, keepdims=True)
    rest = jnp.broadcast_to(half, (16, half.shape[1]))
    at = lax.broadcasted_iota(jnp.int32, rest.shape, 0)
    rows = jnp.zeros_like(rest)
    for k in range(3):
        piece = rest.astype(BF16).astype(F32)
        rest = rest - piece
        rows = jnp.where(at == k, -piece, rows)
    return rows


def unit_rows(width):
    at = lax.broadcasted_iota(jnp.int32, (16, width), 0)
    return jnp.where(at < 3, 1.0, 0.0)


def lower_inverse(spread):
    n = spread.shape[0]
    at_row = lax.broadcasted_iota(jnp.int32, (n, 2 * n), 0)
    at_col = lax.broadcasted_iota(jnp.int32, (n, 2 * n), 1)
    both = jnp.concatenate([spread, spread], axis=1)
    work = jnp.where(at_col < n, both, jnp.where(at_col - n == at_row, 1.0, 0.0))
    for k in range(n):
        pivot_row = work[k : k + 1, :]
        inverse = lax.rsqrt(work[k : k + 1, k : k + 1])
        pivot_row = pivot_row * inverse
        column = work[:, k : k + 1] * inverse
        work = jnp.where(
            at_row > k, work - column * pivot_row, jnp.where(at_row == k, pivot_row, work)
        )
    return work[:, n:]


NEAR = sorted(
    ((dx, dy) for dx in range(4) for dy in range(4)),
    key=lambda o: min(o[0], 4 - o[0]) + min(o[1], 4 - o[1]),
)
PAIRS = ((2, -1), (1, 0), (4, -3), (3, -2), (8, -7), (7, -6), (6, -5), (5, -4))
REACH = 4


def kernel(
    desc_ref, dens_ref, vec_ref, out_ref,
    src, feats, tgt, wts, acc, parts_out, parts_in, slices_in, sums_in, total_in,
    src_s, src_r, sib_s, sib_r, tgt_s, tgt_r, part_s, part_r, ga_s, ga_r, gb_s, gb_r, gc_s, gc_r,
):
    row, z = lax.axis_index("row"), lax.axis_index("col")
    p, c = row // 2, row % 2
    px, py = p // 4, p % 4
    other = 1 - c
    half = p // 8
    samples = float(BLOCK * PLANE * DEPTH * 2)

    def chip(dx, dy):
        return ((px + dx) % 4) * 4 + (py + dy) % 4

    def along(d):
        return (z + d + DEPTH) % DEPTH

    barrier = pltpu.get_barrier_semaphore()

    def greet(device):
        pl.semaphore_signal(barrier, inc=1, device_id=device, device_id_type=MESH)

    for d in range(1, REACH + 1):
        greet((row, along(d)))
        greet((row, along(-d)))
    for dx, dy in NEAR[1:]:
        greet((chip(dx, dy) * 2 + c, z))
    greet((p * 2 + other, z))

    lane16 = lax.broadcasted_iota(jnp.int32, (16, 128), 1)
    at16 = lax.broadcasted_iota(jnp.int32, (16, 128), 0)
    turn = lambda v: pltpu.roll(v, 64, 1)
    pad = lambda v: jnp.concatenate([v, jnp.zeros((v.shape[0], 256 - BLOCK), v.dtype)], axis=1)

    def fold(v):
        return jnp.where(lane16 < 64, v[:16], turn(v[16:]))

    def merge(first, second):
        return jnp.concatenate(
            [jnp.where(lane16 < 64, first, turn(second)), jnp.where(lane16 < 64, turn(first), second)],
            axis=0,
        )

    x = pad(desc_ref[...].astype(F32))
    feats[7, 0:32] = x[:, :128].astype(BF16)
    feats[7, 32:48] = fold(x[:, 128:]).astype(BF16)
    source = jnp.concatenate([x, norm_rows(x), unit_rows(256)], axis=0)
    later = pltpu.roll(source, 160, 1)
    packed = jnp.concatenate([source[:, :128], later[:, :128]], axis=0).T[:96]
    src[0, 0, 0:96] = packed.astype(BF16)
    vec = vec_ref[...]
    inverse = pad(1.0 / dens_ref[...])
    weighted = pad(vec / dens_ref[...])
    src[0, 0, 96:128] = weighted[:, :128].astype(BF16)
    src[0, 0, 128:144] = fold(weighted[:, 128:]).astype(BF16)
    tail = jnp.broadcast_to(inverse[:, 128:], (16, 128))
    src[0, 0, 144:160] = jnp.where(
        at16 == 0,
        jnp.broadcast_to(inverse[:, :128], (16, 128)),
        jnp.where(at16 == 1, jnp.where(lane16 < 64, tail, turn(tail)), 0.0),
    ).astype(BF16)

    pl.semaphore_wait(barrier, 2 * REACH + 16)

    def remote(source_ref, target_ref, send_sem, recv_sem, device):
        return pltpu.make_async_remote_copy(
            src_ref=source_ref, dst_ref=target_ref, send_sem=send_sem, recv_sem=recv_sem,
            device_id=device, device_id_type=MESH,
        )

    def src_copy(j):
        return remote(
            src.at[0, 0], src.at[0, j], src_s.at[j], src_r.at[j], (chip(*NEAR[j]) * 2 + c, z)
        )

    def sib_copy(j):
        return remote(
            src.at[0, j], src.at[1, j], sib_s.at[j], sib_r.at[j], (p * 2 + other, z)
        )

    def tgt_copy(e):
        if abs(e) <= REACH:
            return remote(
                feats.at[7], feats.at[7 + e], tgt_s.at[7 + e], tgt_r.at[7 + e], (row, along(-e))
            )
        step = REACH if e > 0 else -REACH
        return remote(
            feats.at[7 + e - step], feats.at[7 + e], tgt_s.at[7 + e], tgt_r.at[7 + e],
            (row, along(-step)),
        )

    near = [e for d in range(1, REACH + 1) for e in (d, -d)]
    far = [e for d in range(1, REACH + 1) for e in (d + REACH, -d - REACH) if e > -8]
    for e in near:
        tgt_copy(e).start()
    sib_copy(0).start()
    for j in range(1, 16):
        src_copy(j).start()
    acc[...] = jnp.zeros_like(acc)
    for e in near:
        tgt_copy(e).wait_recv()
        ahead = e + (REACH if e > 0 else -REACH)
        if ahead in far:
            tgt_copy(ahead).start()

    unit_tile = unit_rows(128)
    zeros = jnp.zeros((64, 128), F32)

    def build(pair):
        first, second = (feats[7 + e].astype(F32) for e in PAIRS[pair])
        for t, tile in enumerate((first[:32], second[:32], merge(first[32:], second[32:]))):
            rows = jnp.concatenate([tile, unit_tile, norm_rows(tile)], axis=0)
            k = 3 * pair + t
            at = slice(128 * (k % 2), 128 * (k % 2) + 128)
            tgt[0, k // 2, :, at] = jnp.concatenate([rows, zeros], axis=0).astype(BF16)
            tgt[1, k // 2, :, at] = jnp.concatenate([zeros, rows], axis=0).astype(BF16)

    for pair in range(4):
        build(pair)

    def columns(j):
        first, second = src[0, j], src[1, j]
        wts[j, :, 0:128] = jnp.concatenate([first[96:128], first[144:160]], axis=0)
        wts[j, :, 128:256] = jnp.concatenate([second[96:128], second[144:160]], axis=0)
        tails = merge(first[128:144].astype(F32), second[128:144].astype(F32))
        ends = jnp.where(
            lane16 < 64, first[144:160].astype(F32), second[144:160].astype(F32)
        )
        ends = jnp.where(at16 == 0, jnp.broadcast_to(ends[1:2], (16, 128)), 0.0)
        wts[j, :, 256:384] = jnp.concatenate([tails, ends], axis=0).astype(BF16)

    def work(first_chunk, m):
        units = [(k, n) for k in range(6) for n in range(2)]
        inner, kernels = {}, {}
        for i in range(len(units) + 2):
            if i < len(units):
                k, n = units[i]
                rows = jnp.concatenate(
                    [src[s, 4 * m + 2 * n + j, 0:96] for j in range(2) for s in range(2)], axis=0
                )
                inner[i] = [
                    jnp.dot(rows, tgt[v, first_chunk + k], preferred_element_type=F32)
                    for v in range(2)
                ]
            if 0 <= i - 1 < len(units):
                low, high = (
                    jnp.exp2(u * F32(EXPONENT)).astype(BF16) for u in inner.pop(i - 1)
                )
                order = []
                for j in range(2):
                    a, b = 192 * j, 192 * j + 96
                    order += [
                        low[a : a + 96], high[a : a + 32], low[b : b + 96], high[b : b + 32],
                        high[a + 32 : a + 96], high[b + 32 : b + 96],
                    ]
                kernels[i - 1] = jnp.concatenate(order, axis=0)
            if 0 <= i - 2 < len(units):
                k, n = units[i - 2]
                weights = jnp.concatenate(
                    [wts[4 * m + 2 * n + j] for j in range(2)], axis=1
                )
                acc[first_chunk + k] += jnp.dot(
                    weights, kernels.pop(i - 2), preferred_element_type=F32
                )

    def part_copy(e):
        return remote(
            parts_out.at[7 + e], parts_in.at[7 + e], part_s.at[7 + e], part_r.at[7 + e],
            (row, along(e)),
        )

    def send_parts(pair):
        tiles = [
            acc[k // 2, :, 128 * (k % 2) : 128 * (k % 2) + 128]
            for k in range(3 * pair, 3 * pair + 3)
        ]
        both = tiles[2]
        for s, e in enumerate(PAIRS[pair]):
            tail = turn(both) if s else both
            parts_out[7 + e, 0:32] = tiles[s][:32].astype(BF16)
            parts_out[7 + e, 32:48] = fold(tail[:32]).astype(BF16)
            parts_out[7 + e, 48:64] = jnp.where(
                at16 == 0,
                jnp.broadcast_to(tiles[s][32:33], (16, 128)),
                jnp.broadcast_to(tail[32:33], (16, 128)),
            ).astype(BF16)
            if e != 0:
                part_copy(e).start()

    def arrive(m):
        for j in range(4 * m, 4 * m + 4):
            if j > 0:
                src_copy(j).wait_recv()
                sib_copy(j).start()

    arrive(0)
    for m in range(4):
        if m < 3:
            arrive(m + 1)
        for j in range(4 * m, 4 * m + 4):
            sib_copy(j).wait_recv()
            columns(j)
        work(0, m)
    for pair in range(4):
        send_parts(pair)
    for e in far:
        tgt_copy(e).wait_recv()
    for pair in range(4, 8):
        build(pair)

    def second(m, _):
        work(6, m)
        return 0

    lax.fori_loop(0, 4, second, 0)
    for pair in range(4, 8):
        send_parts(pair)
    sums = parts_out[7].astype(F32)
    ups = [e for pair in PAIRS for e in pair if e != 0]
    for e in ups:
        part_copy(e).wait_recv()
        sums = sums + parts_in[7 + e].astype(F32)
    tail = sums[32:48]
    tail = jnp.concatenate([tail, turn(tail)], axis=0)
    top = jnp.concatenate([sums[:32], tail], axis=1)[:, :BLOCK]
    degree = jnp.concatenate([sums[48:49], sums[49:50]], axis=1)[:, :BLOCK]
    diffused = top / degree

    stacked = jnp.concatenate([vec, diffused], axis=0)
    gram = lax.dot_general(
        stacked, stacked, (((1,), (1,)), ((), ())), precision=HIGHEST, preferred_element_type=F32
    )
    gram = jnp.concatenate([gram, jnp.zeros((64, 64), F32)], axis=1)
    slices = slices_in.at[1]
    for j in range(8):
        slices[j] = gram[8 * j : 8 * j + 8]

    def ga_copy(k):
        q = (p + k) % PLANE
        return pltpu.make_async_remote_copy(
            src_ref=slices_in.at[1, q % 8], dst_ref=slices_in.at[0, k],
            send_sem=ga_s.at[k], recv_sem=ga_r.at[k],
            device_id=(q * 2 + c, z), device_id_type=MESH,
        )

    def send_ga(k, _):
        ga_copy(k).start()
        return 0

    lax.fori_loop(1, 16, send_ga, 0)
    part = slices_in[1, p % 8]
    for k in range(1, 16):
        ga_copy(k).wait_recv()
        part = part + slices_in[0, k]
    sums_in[0] = part

    def gb_copy(k):
        return pltpu.make_async_remote_copy(
            src_ref=sums_in.at[0], dst_ref=sums_in.at[k],
            send_sem=gb_s.at[k], recv_sem=gb_r.at[k],
            device_id=(row, (z + k) % DEPTH), device_id_type=MESH,
        )

    def send_gb(k, _):
        gb_copy(k).start()
        return 0

    lax.fori_loop(1, 16, send_gb, 0)
    for k in range(1, 16):
        gb_copy(k).wait_recv()
        part = part + sums_in[k]

    mine = p % 8
    total_in[c, mine] = part

    def gc_copy(s, k):
        q = half * 8 + (mine + k) % 8
        core = c if s == 0 else other
        return pltpu.make_async_remote_copy(
            src_ref=total_in.at[c, mine], dst_ref=total_in.at[c, mine],
            send_sem=gc_s.at[s, k], recv_sem=gc_r.at[s, k],
            device_id=(q * 2 + core, z), device_id_type=MESH,
        )

    def gc_recv(s, k):
        slot = (mine + 8 - k) % 8
        core = c if s == 0 else other
        return pltpu.make_async_remote_copy(
            src_ref=total_in.at[core, slot], dst_ref=total_in.at[core, slot],
            send_sem=gc_s.at[s, k], recv_sem=gc_r.at[s, k],
            device_id=(row, z), device_id_type=MESH,
        )

    def send_gc(k, _):
        gc_copy(1, k).start()

        @pl.when(k > 0)
        def _():
            gc_copy(0, k).start()

        return 0

    lax.fori_loop(0, 8, send_gc, 0)

    def wait_gc(k, _):
        gc_recv(1, k).wait_recv()

        @pl.when(k > 0)
        def _():
            gc_recv(0, k).wait_recv()

        return 0

    lax.fori_loop(0, 8, wait_gc, 0)
    total = (total_in[0] + total_in[1]).reshape(64, 128)
    basis, coupling, square = total[:32, :32], total[:32, 32:64], total[32:, 32:64]
    dot_t = lambda a, b: lax.dot_general(
        a, b, (((0,), (0,)), ((), ())), precision=HIGHEST, preferred_element_type=F32
    )
    mixed = jnp.dot(basis, coupling, precision=HIGHEST, preferred_element_type=F32)
    spread = square + dot_t(
        coupling, mixed * (1.0 / (samples * samples)) - coupling * (2.0 / samples)
    )
    remainder = diffused - dot_t(coupling, vec) * (1.0 / samples)
    factor = lower_inverse(spread)
    out_ref[...] = math.sqrt(samples) * jnp.dot(
        factor, remainder, precision=HIGHEST, preferred_element_type=F32
    )

    for j in range(1, 16):
        src_copy(j).wait_send()
    for j in range(16):
        sib_copy(j).wait_send()
    for e in near + far:
        tgt_copy(e).wait_send()
    for e in ups:
        part_copy(e).wait_send()

    def wait_sent(k, _):
        ga_copy(k).wait_send()
        gb_copy(k).wait_send()
        return 0

    lax.fori_loop(1, 16, wait_sent, 0)

    def wait_gc_sent(k, _):
        gc_copy(1, k).wait_send()

        @pl.when(k > 0)
        def _():
            gc_copy(0, k).wait_send()

        return 0

    lax.fori_loop(0, 8, wait_gc_sent, 0)


def per_device(descriptors, densities, vectors):
    dma = pltpu.SemaphoreType.DMA
    return pl.pallas_call(
        kernel,
        out_shape=jax.ShapeDtypeStruct((32, BLOCK), F32),
        in_specs=[pl.BlockSpec(memory_space=pltpu.VMEM)] * 3,
        out_specs=pl.BlockSpec(memory_space=pltpu.VMEM),
        scratch_shapes=[
            pltpu.VMEM((2, 16, 160, 128), BF16),
            pltpu.VMEM((16, 48, 128), BF16),
            pltpu.VMEM((2, 12, 128, 256), BF16),
            pltpu.VMEM((16, 48, 384), BF16),
            pltpu.VMEM((12, 48, 256), F32),
            pltpu.VMEM((16, 64, 128), BF16),
            pltpu.VMEM((16, 64, 128), BF16),
            pltpu.VMEM((2, 16, 8, 128), F32),
            pltpu.VMEM((16, 8, 128), F32),
            pltpu.VMEM((2, 8, 8, 128), F32),
            *([dma((16,))] * 12),
            dma((2, 8)), dma((2, 8)),
        ],
        compiler_params=pltpu.CompilerParams(
            collective_id=0, has_side_effects=True, vmem_limit_bytes=48 << 20
        ),
    )(descriptors, densities.reshape(1, BLOCK), vectors)


def solution(mesh):
    placed = P(None, ("row", "col"))
    return jax.shard_map(
        per_device,
        mesh=mesh,
        in_specs=(placed, P(("row", "col")), placed),
        out_specs=placed,
        check_vma=False,
    )
```

time: 85.3 us -> 79.3 us (0.930)
  Pallas kernels: 82.3 us -> 76.3 us
    pallas_call x1, Pallas kernels: 82.3 us -> 76.3 us  [per_device(): pl.pallas_call(kernel, out_shape=jax.ShapeDtypeStruct((32, BLOCK), F32),...]
where the time goes in v2:
time: 79.3 us; the launch traced here: 79.1 us
  Pallas kernels  76.3 us (96%)
  local copies, waits for them, and re-layouts  2.77 us (3%)
    pallas_call x1, Pallas kernels, per_device(): pl.pallas_call(kernel, out_shape=jax.ShapeDtypeStruct((32, BLOCK), F32),...  76.3 us
    unnamed x7, local copies, waits for them, and re-layouts  2.77 us

profile of v2, /device:TPU:1, one launch (start us, length us, event | category | flops | bytes accessed | tf_op | source)
XLA Modules:
  0.0 79.1 jit_solution(14466327555382145593)
XLA Ops:
  0.0 0.0 copy-start.2
  0.0 0.7 copy-done.2
  0.7 0.0 copy-start
  0.7 0.8 copy-done
  1.4 0.0 copy-start.1
  1.4 0.7 copy-done.1
  2.2 76.3 %shard_map.37 = f32[32,192]{1,0:T(8,128)S(1)} custom-call(bf16[32,192]{1,0:T(8,128)(2,1)S(1)} %copy-done.1, f32[1,192]{1,0:T(1,128)S(1)} %bitcast.1, f32[32,192]{1,0:T(8,128)S(1)} %copy-done), custom_call_target="tpu_custom_call" | custom-call | tf_op jit(solution)/shard_map/pallas_call | solution.py:423
  78.5 0.6 copy.5
Async XLA Ops:
  0.0 0.7 copy-start.2
  0.7 0.8 copy-start
  1.4 0.7 copy-start.1

commit v3 on v2

--- a/solution.py
+++ b/solution.py
@@ -56,20 +56,29 @@
     ((dx, dy) for dx in range(4) for dy in range(4)),
     key=lambda o: min(o[0], 4 - o[0]) + min(o[1], 4 - o[1]),
 )
-PAIRS = ((2, -1), (1, 0), (4, -3), (3, -2), (8, -7), (7, -6), (6, -5), (5, -4))
+PAIRS = ((4, -3), (3, -2), (8, -7), (7, -6), (6, -5), (5, -4), (2, -1), (1, 0))
 REACH = 4
 
 
 def kernel(
-    desc_ref, dens_ref, vec_ref, out_ref,
-    src, feats, tgt, wts, acc, parts_out, parts_in, slices_in, sums_in, total_in,
-    src_s, src_r, sib_s, sib_r, tgt_s, tgt_r, part_s, part_r, ga_s, ga_r, gb_s, gb_r, gc_s, gc_r,
+    desc_hbm, dens_hbm, vec_hbm, out_ref,
+    desc_ref, dens_ref, vec_ref, src, feats, tgt, wts, acc, parts_out, parts_in,
+    basis_out, basis_plane, basis_z, basis_sib, gram_out, gram_plane, gram_z, gram_sib,
+    in_s, src_s, src_r, sib_s, sib_r, tgt_s, tgt_r, part_s, part_r,
+    bp_s, bp_r, bz_s, bz_r, gp_s, gp_r, gz_s, gz_r, one_s, one_r,
 ):
+    loads = [
+        pltpu.make_async_copy(there, here, in_s.at[k])
+        for k, (there, here) in enumerate(
+            ((desc_hbm, desc_ref), (dens_hbm, dens_ref), (vec_hbm, vec_ref))
+        )
+    ]
+    for load in loads:
+        load.start()
     row, z = lax.axis_index("row"), lax.axis_index("col")
     p, c = row // 2, row % 2
     px, py = p // 4, p % 4
     other = 1 - c
-    half = p // 8
     samples = float(BLOCK * PLANE * DEPTH * 2)
 
     def chip(dx, dy):
@@ -103,6 +112,14 @@
             [jnp.where(lane16 < 64, first, turn(second)), jnp.where(lane16 < 64, turn(first), second)],
             axis=0,
         )
+
+    for load in loads:
+        load.wait()
+    def wide(v):
+        return jnp.concatenate([v[8 * g : 8 * g + 8] for g in range(4)], axis=1)
+
+    def square(v):
+        return jnp.concatenate([v[:, 32 * g : 32 * g + 32] for g in range(4)], axis=0)
 
     x = pad(desc_ref[...].astype(F32))
     feats[7, 0:32] = x[:, :128].astype(BF16)
@@ -123,6 +140,11 @@
         jnp.where(at16 == 1, jnp.where(lane16 < 64, tail, turn(tail)), 0.0),
     ).astype(BF16)
 
+    basis_out[0] = wide(
+        lax.dot_general(
+            vec, vec, (((1,), (1,)), ((), ())), precision=HIGHEST, preferred_element_type=F32
+        )
+    )
     pl.semaphore_wait(barrier, 2 * REACH + 16)
 
     def remote(source_ref, target_ref, send_sem, recv_sem, device):
@@ -152,6 +174,29 @@
             (row, along(-step)),
         )
 
+    def plane_copy(here, there, sends, receives, j):
+        return remote(
+            here.at[0], there.at[j], sends.at[j], receives.at[j], (chip(*NEAR[j]) * 2 + c, z)
+        )
+
+    def z_copy(here, there, sends, receives, k):
+        return remote(here.at[1], there.at[k], sends.at[k], receives.at[k], (row, along(k)))
+
+    def sib_one(here, there, k):
+        return remote(here, there, one_s.at[k], one_r.at[k], (p * 2 + other, z))
+
+    basis_p = functools.partial(plane_copy, basis_out, basis_plane, bp_s, bp_r)
+    basis_a = functools.partial(z_copy, basis_out, basis_z, bz_s, bz_r)
+    gram_p = functools.partial(plane_copy, gram_out, gram_plane, gp_s, gp_r)
+    gram_a = functools.partial(z_copy, gram_out, gram_z, gz_s, gz_r)
+
+    def collect(copy, own, slots):
+        total = own
+        for k in range(1, 16):
+            copy(k).wait_recv()
+            total = total + slots[k]
+        return total
+
     near = [e for d in range(1, REACH + 1) for e in (d, -d)]
     far = [e for d in range(1, REACH + 1) for e in (d + REACH, -d - REACH) if e > -8]
     for e in near:
@@ -159,6 +204,8 @@
     sib_copy(0).start()
     for j in range(1, 16):
         src_copy(j).start()
+    for j in range(1, 16):
+        basis_p(j).start()
     acc[...] = jnp.zeros_like(acc)
     for e in near:
         tgt_copy(e).wait_recv()
@@ -178,7 +225,7 @@
             tgt[0, k // 2, :, at] = jnp.concatenate([rows, zeros], axis=0).astype(BF16)
             tgt[1, k // 2, :, at] = jnp.concatenate([zeros, rows], axis=0).astype(BF16)
 
-    for pair in range(4):
+    for pair in range(2):
         build(pair)
 
     def columns(j):
@@ -192,14 +239,14 @@
         ends = jnp.where(at16 == 0, jnp.broadcast_to(ends[1:2], (16, 128)), 0.0)
         wts[j, :, 256:384] = jnp.concatenate([tails, ends], axis=0).astype(BF16)
 
-    def work(first_chunk, m):
-        units = [(k, n) for k in range(6) for n in range(2)]
+    def work(first_chunk, first_chip, pairs):
+        units = [(k, n) for k in range(3) for n in range(pairs)]
         inner, kernels = {}, {}
         for i in range(len(units) + 2):
             if i < len(units):
                 k, n = units[i]
                 rows = jnp.concatenate(
-                    [src[s, 4 * m + 2 * n + j, 0:96] for j in range(2) for s in range(2)], axis=0
+                    [src[s, first_chip + 2 * n + j, 0:96] for j in range(2) for s in range(2)], axis=0
                 )
                 inner[i] = [
                     jnp.dot(rows, tgt[v, first_chunk + k], preferred_element_type=F32)
@@ -220,7 +267,7 @@
             if 0 <= i - 2 < len(units):
                 k, n = units[i - 2]
                 weights = jnp.concatenate(
-                    [wts[4 * m + 2 * n + j] for j in range(2)], axis=1
+                    [wts[first_chip + 2 * n + j] for j in range(2)], axis=1
                 )
                 acc[first_chunk + k] += jnp.dot(
                     weights, kernels.pop(i - 2), preferred_element_type=F32
@@ -263,21 +310,28 @@
         for j in range(4 * m, 4 * m + 4):
             sib_copy(j).wait_recv()
             columns(j)
-        work(0, m)
-    for pair in range(4):
+        work(0, 4 * m, 2)
+    for pair in range(2):
         send_parts(pair)
     for e in far:
         tgt_copy(e).wait_recv()
-    for pair in range(4, 8):
-        build(pair)
-
-    def second(m, _):
-        work(6, m)
-        return 0
-
-    lax.fori_loop(0, 4, second, 0)
-    for pair in range(4, 8):
-        send_parts(pair)
+    basis_out[1] = collect(basis_p, basis_out[0], basis_plane)
+    for k in range(1, 16):
+        basis_a(k).start()
+    for group in range(1, 4):
+        for pair in (2 * group, 2 * group + 1):
+            build(pair)
+
+        def rest(m, _):
+            work(3 * group, 8 * m, 4)
+            return 0
+
+        lax.fori_loop(0, 2, rest, 0)
+        for pair in (2 * group, 2 * group + 1):
+            send_parts(pair)
+        if group == 2:
+            basis_out[2] = collect(basis_a, basis_out[1], basis_z)
+            sib_one(basis_out.at[2], basis_sib, 0).start()
     sums = parts_out[7].astype(F32)
     ups = [e for pair in PAIRS for e in pair if e != 0]
     for e in ups:
@@ -289,99 +343,35 @@
     degree = jnp.concatenate([sums[48:49], sums[49:50]], axis=1)[:, :BLOCK]
     diffused = top / degree
 
-    stacked = jnp.concatenate([vec, diffused], axis=0)
-    gram = lax.dot_general(
-        stacked, stacked, (((1,), (1,)), ((), ())), precision=HIGHEST, preferred_element_type=F32
-    )
-    gram = jnp.concatenate([gram, jnp.zeros((64, 64), F32)], axis=1)
-    slices = slices_in.at[1]
-    for j in range(8):
-        slices[j] = gram[8 * j : 8 * j + 8]
-
-    def ga_copy(k):
-        q = (p + k) % PLANE
-        return pltpu.make_async_remote_copy(
-            src_ref=slices_in.at[1, q % 8], dst_ref=slices_in.at[0, k],
-            send_sem=ga_s.at[k], recv_sem=ga_r.at[k],
-            device_id=(q * 2 + c, z), device_id_type=MESH,
-        )
-
-    def send_ga(k, _):
-        ga_copy(k).start()
-        return 0
-
-    lax.fori_loop(1, 16, send_ga, 0)
-    part = slices_in[1, p % 8]
+    dot_c = lambda a, b: lax.dot_general(
+        a, b, (((1,), (1,)), ((), ())), precision=HIGHEST, preferred_element_type=F32
+    )
+    grams = (wide(dot_c(vec, diffused)), wide(dot_c(diffused, diffused)))
+    first = c == 0
+    gram_out[3] = jnp.where(first, grams[1], grams[0])
+    swap = sib_one(gram_out.at[3], gram_sib.at[0], 1)
+    swap.start()
+    swap.wait_recv()
+    gram_out[0] = jnp.where(first, grams[0], grams[1]) + gram_sib[0]
     for k in range(1, 16):
-        ga_copy(k).wait_recv()
-        part = part + slices_in[0, k]
-    sums_in[0] = part
-
-    def gb_copy(k):
-        return pltpu.make_async_remote_copy(
-            src_ref=sums_in.at[0], dst_ref=sums_in.at[k],
-            send_sem=gb_s.at[k], recv_sem=gb_r.at[k],
-            device_id=(row, (z + k) % DEPTH), device_id_type=MESH,
-        )
-
-    def send_gb(k, _):
-        gb_copy(k).start()
-        return 0
-
-    lax.fori_loop(1, 16, send_gb, 0)
+        gram_p(k).start()
+    gram_out[1] = collect(gram_p, gram_out[0], gram_plane)
     for k in range(1, 16):
-        gb_copy(k).wait_recv()
-        part = part + sums_in[k]
-
-    mine = p % 8
-    total_in[c, mine] = part
-
-    def gc_copy(s, k):
-        q = half * 8 + (mine + k) % 8
-        core = c if s == 0 else other
-        return pltpu.make_async_remote_copy(
-            src_ref=total_in.at[c, mine], dst_ref=total_in.at[c, mine],
-            send_sem=gc_s.at[s, k], recv_sem=gc_r.at[s, k],
-            device_id=(q * 2 + core, z), device_id_type=MESH,
-        )
-
-    def gc_recv(s, k):
-        slot = (mine + 8 - k) % 8
-        core = c if s == 0 else other
-        return pltpu.make_async_remote_copy(
-            src_ref=total_in.at[core, slot], dst_ref=total_in.at[core, slot],
-            send_sem=gc_s.at[s, k], recv_sem=gc_r.at[s, k],
-            device_id=(row, z), device_id_type=MESH,
-        )
-
-    def send_gc(k, _):
-        gc_copy(1, k).start()
-
-        @pl.when(k > 0)
-        def _():
-            gc_copy(0, k).start()
-
-        return 0
-
-    lax.fori_loop(0, 8, send_gc, 0)
-
-    def wait_gc(k, _):
-        gc_recv(1, k).wait_recv()
-
-        @pl.when(k > 0)
-        def _():
-            gc_recv(0, k).wait_recv()
-
-        return 0
-
-    lax.fori_loop(0, 8, wait_gc, 0)
-    total = (total_in[0] + total_in[1]).reshape(64, 128)
-    basis, coupling, square = total[:32, :32], total[:32, 32:64], total[32:, 32:64]
+        gram_a(k).start()
+    sib_one(basis_out.at[2], basis_sib, 0).wait_recv()
+    basis = square(basis_out[2] + basis_sib[...])
+    gram_out[2] = collect(gram_a, gram_out[1], gram_z)
+    swap_back = sib_one(gram_out.at[2], gram_sib.at[1], 2)
+    swap_back.start()
+    swap_back.wait_recv()
+    mine, others = gram_out[2], gram_sib[1]
+    coupling = square(jnp.where(first, mine, others))
+    diffused_gram = square(jnp.where(first, others, mine))
     dot_t = lambda a, b: lax.dot_general(
         a, b, (((0,), (0,)), ((), ())), precision=HIGHEST, preferred_element_type=F32
     )
     mixed = jnp.dot(basis, coupling, precision=HIGHEST, preferred_element_type=F32)
-    spread = square + dot_t(
+    spread = diffused_gram + dot_t(
         coupling, mixed * (1.0 / (samples * samples)) - coupling * (2.0 / samples)
     )
     remainder = diffused - dot_t(coupling, vec) * (1.0 / samples)
@@ -399,23 +389,12 @@
     for e in ups:
         part_copy(e).wait_send()
 
-    def wait_sent(k, _):
-        ga_copy(k).wait_send()
-        gb_copy(k).wait_send()
-        return 0
-
-    lax.fori_loop(1, 16, wait_sent, 0)
-
-    def wait_gc_sent(k, _):
-        gc_copy(1, k).wait_send()
-
-        @pl.when(k > 0)
-        def _():
-            gc_copy(0, k).wait_send()
-
-        return 0
-
-    lax.fori_loop(0, 8, wait_gc_sent, 0)
+    for k in range(1, 16):
+        for copy in (basis_p, basis_a, gram_p, gram_a):
+            copy(k).wait_send()
+    sib_one(basis_out.at[2], basis_sib, 0).wait_send()
+    swap.wait_send()
+    swap_back.wait_send()
 
 
 def per_device(descriptors, densities, vectors):
@@ -423,9 +402,12 @@
     return pl.pallas_call(
         kernel,
         out_shape=jax.ShapeDtypeStruct((32, BLOCK), F32),
-        in_specs=[pl.BlockSpec(memory_space=pltpu.VMEM)] * 3,
+        in_specs=[pl.BlockSpec(memory_space=pl.ANY)] * 3,
         out_specs=pl.BlockSpec(memory_space=pltpu.VMEM),
         scratch_shapes=[
+            pltpu.VMEM((32, BLOCK), BF16),
+            pltpu.VMEM((1, BLOCK), F32),
+            pltpu.VMEM((32, BLOCK), F32),
             pltpu.VMEM((2, 16, 160, 128), BF16),
             pltpu.VMEM((16, 48, 128), BF16),
             pltpu.VMEM((2, 12, 128, 256), BF16),
@@ -433,14 +415,20 @@
             pltpu.VMEM((12, 48, 256), F32),
             pltpu.VMEM((16, 64, 128), BF16),
             pltpu.VMEM((16, 64, 128), BF16),
-            pltpu.VMEM((2, 16, 8, 128), F32),
+            pltpu.VMEM((3, 8, 128), F32),
             pltpu.VMEM((16, 8, 128), F32),
-            pltpu.VMEM((2, 8, 8, 128), F32),
-            *([dma((16,))] * 12),
-            dma((2, 8)), dma((2, 8)),
+            pltpu.VMEM((16, 8, 128), F32),
+            pltpu.VMEM((8, 128), F32),
+            pltpu.VMEM((4, 8, 128), F32),
+            pltpu.VMEM((16, 8, 128), F32),
+            pltpu.VMEM((16, 8, 128), F32),
+            pltpu.VMEM((2, 8, 128), F32),
+            dma((3,)),
+            *([dma((16,))] * 16),
+            dma((3,)), dma((3,)),
         ],
         compiler_params=pltpu.CompilerParams(
-            collective_id=0, has_side_effects=True, vmem_limit_bytes=48 << 20
+            collective_id=0, has_side_effects=True, vmem_limit_bytes=63 << 20
         ),
     )(descriptors, densities.reshape(1, BLOCK), vectors)
 

time: 79.3 us -> 69.7 us (0.88)
  Pallas kernels: 76.3 us -> 67.9 us
  local copies, waits for them, and re-layouts: 2.77 us -> 1.38 us
    pallas_call x1, Pallas kernels: 76.3 us -> 67.9 us  [per_device(): pl.pallas_call(kernel, out_shape=jax.ShapeDtypeStruct((32, BLOCK), F32),...]
    unnamed x7 -> x1, local copies, waits for them, and re-layouts: 2.77 us -> 1.38 us
where the time goes in v3:
time: 69.7 us; the launch traced here: 69.3 us
  Pallas kernels  67.9 us (97%)
  local copies, waits for them, and re-layouts  1.38 us (2%)
    pallas_call x1, Pallas kernels, per_device(): pl.pallas_call(kernel, out_shape=jax.ShapeDtypeStruct((32, BLOCK), F32),...  67.9 us

profile of v3, /device:TPU:1, one launch (start us, length us, event | category | flops | bytes accessed | tf_op | source)
XLA Modules:
  0.0 69.3 jit_solution(13027024458805974800)
XLA Ops:
  0.0 67.9 %shard_map.37 = f32[32,192]{1,0:T(8,128)} custom-call(bf16[32,192]{1,0:T(8,128)(2,1)} %desc_hbm.1, f32[1,192]{1,0:T(1,128)} %bitcast.1, f32[32,192]{1,0:T(8,128)} %vec_hbm.1), custom_call_target="tpu_custom_call" | custom-call | tf_op jit(solution)/shard_map/pallas_call | solution.py:402
  67.9 1.4 %copy.5 = f32[32,192]{1,0:T(8,128)} copy(f32[32,192]{1,0:T(8,128)} %shard_map.37) | data formatting | bytes 49152

commit v4 on v3

--- a/solution.py
+++ b/solution.py
@@ -36,20 +36,25 @@
 
 
 def lower_inverse(spread):
-    n = spread.shape[0]
-    at_row = lax.broadcasted_iota(jnp.int32, (n, 2 * n), 0)
-    at_col = lax.broadcasted_iota(jnp.int32, (n, 2 * n), 1)
+    n, step = spread.shape[0], 4
+    shape = (n, 2 * n)
+    at_row = lax.broadcasted_iota(jnp.int32, shape, 0)
+    at_col = lax.broadcasted_iota(jnp.int32, shape, 1)
     both = jnp.concatenate([spread, spread], axis=1)
     work = jnp.where(at_col < n, both, jnp.where(at_col - n == at_row, 1.0, 0.0))
-    for k in range(n):
-        pivot_row = work[k : k + 1, :]
-        inverse = lax.rsqrt(work[k : k + 1, k : k + 1])
-        pivot_row = pivot_row * inverse
-        column = work[:, k : k + 1] * inverse
-        work = jnp.where(
-            at_row > k, work - column * pivot_row, jnp.where(at_row == k, pivot_row, work)
-        )
-    return work[:, n:]
+    finished = []
+    for k in range(0, n, step):
+        rows = [work[k + i : k + i + 1] for i in range(step)]
+        columns = [jnp.broadcast_to(work[:, k + i : k + i + 1], shape) for i in range(step)]
+        for i in range(step):
+            pivot = columns[i][k + i : k + i + 1]
+            finished.append(rows[i] * lax.rsqrt(pivot))
+            share = columns[i] * (1.0 / pivot)
+            for j in range(i + 1, step):
+                rows[j] = rows[j] - share[k + j : k + j + 1] * rows[i]
+                columns[j] = columns[j] - share * columns[i][k + j : k + j + 1]
+            work = work - share * rows[i]
+    return jnp.concatenate(finished, axis=0)[:, n:]
 
 
 NEAR = sorted(
@@ -204,8 +209,6 @@
     sib_copy(0).start()
     for j in range(1, 16):
         src_copy(j).start()
-    for j in range(1, 16):
-        basis_p(j).start()
     acc[...] = jnp.zeros_like(acc)
     for e in near:
         tgt_copy(e).wait_recv()
@@ -310,14 +313,14 @@
         for j in range(4 * m, 4 * m + 4):
             sib_copy(j).wait_recv()
             columns(j)
+        if m == 3:
+            for j in range(1, 16):
+                basis_p(j).start()
         work(0, 4 * m, 2)
     for pair in range(2):
         send_parts(pair)
     for e in far:
         tgt_copy(e).wait_recv()
-    basis_out[1] = collect(basis_p, basis_out[0], basis_plane)
-    for k in range(1, 16):
-        basis_a(k).start()
     for group in range(1, 4):
         for pair in (2 * group, 2 * group + 1):
             build(pair)
@@ -329,9 +332,10 @@
         lax.fori_loop(0, 2, rest, 0)
         for pair in (2 * group, 2 * group + 1):
             send_parts(pair)
-        if group == 2:
-            basis_out[2] = collect(basis_a, basis_out[1], basis_z)
-            sib_one(basis_out.at[2], basis_sib, 0).start()
+        if group == 1:
+            basis_out[1] = collect(basis_p, basis_out[0], basis_plane)
+            for k in range(1, 16):
+                basis_a(k).start()
     sums = parts_out[7].astype(F32)
     ups = [e for pair in PAIRS for e in pair if e != 0]
     for e in ups:
@@ -353,10 +357,12 @@
     swap.start()
     swap.wait_recv()
     gram_out[0] = jnp.where(first, grams[0], grams[1]) + gram_sib[0]
-    for k in range(1, 16):
+    for k in range(15, 0, -1):
         gram_p(k).start()
+    basis_out[2] = collect(basis_a, basis_out[1], basis_z)
+    sib_one(basis_out.at[2], basis_sib, 0).start()
     gram_out[1] = collect(gram_p, gram_out[0], gram_plane)
-    for k in range(1, 16):
+    for k in sorted(range(1, 16), key=lambda k: -min(k, DEPTH - k)):
         gram_a(k).start()
     sib_one(basis_out.at[2], basis_sib, 0).wait_recv()
     basis = square(basis_out[2] + basis_sib[...])

time: 69.7 us -> 69.1 us (level)
  no operation moved by 1% of the time
where the time goes in v4:
time: 69.1 us; the launch traced here: 68.8 us
  Pallas kernels  67.4 us (98%)
  local copies, waits for them, and re-layouts  1.38 us (2%)
    pallas_call x1, Pallas kernels, per_device(): pl.pallas_call(kernel, out_shape=jax.ShapeDtypeStruct((32, BLOCK), F32),...  67.4 us

profile of v4, /device:TPU:1, one launch (start us, length us, event | category | flops | bytes accessed | tf_op | source)
XLA Modules:
  0.0 68.8 jit_solution(13350874318863280724)
XLA Ops:
  0.0 67.4 %shard_map.37 = f32[32,192]{1,0:T(8,128)} custom-call(bf16[32,192]{1,0:T(8,128)(2,1)} %desc_hbm.1, f32[1,192]{1,0:T(1,128)} %bitcast.1, f32[32,192]{1,0:T(8,128)} %vec_hbm.1), custom_call_target="tpu_custom_call" | custom-call | tf_op jit(solution)/shard_map/pallas_call | solution.py:408
  67.4 1.4 %copy.5 = f32[32,192]{1,0:T(8,128)} copy(f32[32,192]{1,0:T(8,128)} %shard_map.37) | data formatting | bytes 49152

commit v5 on v4

--- a/solution.py
+++ b/solution.py
@@ -210,6 +210,13 @@
     for j in range(1, 16):
         src_copy(j).start()
     acc[...] = jnp.zeros_like(acc)
+    def arrive(m):
+        for j in range(4 * m, 4 * m + 4):
+            if j > 0:
+                src_copy(j).wait_recv()
+                sib_copy(j).start()
+
+    arrive(0)
     for e in near:
         tgt_copy(e).wait_recv()
         ahead = e + (REACH if e > 0 else -REACH)
@@ -242,8 +249,8 @@
         ends = jnp.where(at16 == 0, jnp.broadcast_to(ends[1:2], (16, 128)), 0.0)
         wts[j, :, 256:384] = jnp.concatenate([tails, ends], axis=0).astype(BF16)
 
-    def work(first_chunk, first_chip, pairs):
-        units = [(k, n) for k in range(3) for n in range(pairs)]
+    def work(first_chunk, first_chip, pairs, chunks=3):
+        units = [(k, n) for k in range(chunks) for n in range(pairs)]
         inner, kernels = {}, {}
         for i in range(len(units) + 2):
             if i < len(units):
@@ -300,13 +307,6 @@
             if e != 0:
                 part_copy(e).start()
 
-    def arrive(m):
-        for j in range(4 * m, 4 * m + 4):
-            if j > 0:
-                src_copy(j).wait_recv()
-                sib_copy(j).start()
-
-    arrive(0)
     for m in range(4):
         if m < 3:
             arrive(m + 1)
@@ -326,12 +326,14 @@
             build(pair)
 
         def rest(m, _):
-            work(3 * group, 8 * m, 4)
+            work(3 * group, 8 * m, 4, 2 if group == 3 else 3)
             return 0
 
         lax.fori_loop(0, 2, rest, 0)
-        for pair in (2 * group, 2 * group + 1):
-            send_parts(pair)
+        send_parts(2 * group)
+        if group == 3:
+            work(3 * group + 2, 0, 8, 1)
+        send_parts(2 * group + 1)
         if group == 1:
             basis_out[1] = collect(basis_p, basis_out[0], basis_plane)
             for k in range(1, 16):

time: 69.1 us -> 68.9 us (level)
  no operation moved by 1% of the time
where the time goes in v5:
time: 68.9 us; the launch traced here: 68.6 us
  Pallas kernels  67.2 us (98%)
  local copies, waits for them, and re-layouts  1.38 us (2%)
    pallas_call x1, Pallas kernels, per_device(): pl.pallas_call(kernel, out_shape=jax.ShapeDtypeStruct((32, BLOCK), F32),...  67.2 us

profile of v5, /device:TPU:1, one launch (start us, length us, event | category | flops | bytes accessed | tf_op | source)
XLA Modules:
  0.0 68.6 jit_solution(6111492386832762190)
XLA Ops:
  0.0 67.2 %shard_map.37 = f32[32,192]{1,0:T(8,128)} custom-call(bf16[32,192]{1,0:T(8,128)(2,1)} %desc_hbm.1, f32[1,192]{1,0:T(1,128)} %bitcast.1, f32[32,192]{1,0:T(8,128)} %vec_hbm.1), custom_call_target="tpu_custom_call" | custom-call | tf_op jit(solution)/shard_map/pallas_call | solution.py:410
  67.3 1.4 %copy.5 = f32[32,192]{1,0:T(8,128)} copy(f32[32,192]{1,0:T(8,128)} %shard_map.37) | data formatting | bytes 49152

commit v6 on v5

--- a/solution.py
+++ b/solution.py
@@ -204,10 +204,12 @@
 
     near = [e for d in range(1, REACH + 1) for e in (d, -d)]
     far = [e for d in range(1, REACH + 1) for e in (d + REACH, -d - REACH) if e > -8]
-    for e in near:
+    for j in range(1, 5):
+        src_copy(j).start()
+    for e in reversed(near):
         tgt_copy(e).start()
     sib_copy(0).start()
-    for j in range(1, 16):
+    for j in range(5, 16):
         src_copy(j).start()
     acc[...] = jnp.zeros_like(acc)
     def arrive(m):

time: 68.9 us -> 68.9 us (level)
  no operation moved by 1% of the time
where the time goes in v6:
time: 68.9 us; the launch traced here: 68.7 us
  Pallas kernels  67.3 us (98%)
  local copies, waits for them, and re-layouts  1.38 us (2%)
    pallas_call x1, Pallas kernels, per_device(): pl.pallas_call(kernel, out_shape=jax.ShapeDtypeStruct((32, BLOCK), F32),...  67.3 us

profile of v6, /device:TPU:1, one launch (start us, length us, event | category | flops | bytes accessed | tf_op | source)
XLA Modules:
  0.0 68.7 jit_solution(9988361737457554158)
XLA Ops:
  0.0 67.3 %shard_map.37 = f32[32,192]{1,0:T(8,128)} custom-call(bf16[32,192]{1,0:T(8,128)(2,1)} %desc_hbm.1, f32[1,192]{1,0:T(1,128)} %bitcast.1, f32[32,192]{1,0:T(8,128)} %vec_hbm.1), custom_call_target="tpu_custom_call" | custom-call | tf_op jit(solution)/shard_map/pallas_call | solution.py:412
  67.3 1.4 %copy.5 = f32[32,192]{1,0:T(8,128)} copy(f32[32,192]{1,0:T(8,128)} %shard_map.37) | data formatting | bytes 49152
